TPU v7x, 32 devices: a whole 2x2x4 slice. The times are simulated.
32 devices in a mesh: group: 2 (over x), expert: 16 (over z, y, core).
Axes of the slice: x: 2, y: 2, z: 4, core: 2. Of those that a mesh axis runs over, the one named last changes fastest.
Arguments:
- source_tokens: bfloat16 [8192, 2048], P(('group', 'expert')), parts along dimension 0, may hold values from -36 to 36
- routes: int32 [8192, 2], P(('group', 'expert')), parts along dimension 0, may hold values from 0 to 3, all different within a row; in each aligned block of 256 rows (0 to 255, 256 to 511, ...) at most 192 rows name the same one
- source_lengths: int32 [32, 4], P(('group', 'expert')), parts along dimension 0, may hold values from 1 to 192, 256 in all within a row
- router_weight: bfloat16 [2048, 4], replicated, may hold values from -0.125 to 0.125
- expert_in: bfloat16 [16, 2048, 1024], P('expert'), may hold values from -0.125 to 0.125
- expert_out: bfloat16 [16, 1024, 2048], P('expert'), may hold values from -0.09375 to 0.09375
- memory_weight: bfloat16 [2048, 2048], replicated, may hold values from -0.125 to 0.125
- decode_inputs: bfloat16 [2, 192, 2048], P(None, ('group', 'expert')), parts along dimension 1, may hold values from -36 to 36
- self_cache: bfloat16 [192, 64, 2048], P(('group', 'expert')), parts along dimension 0, may hold values from -6 to 6
- context_lengths: int32 [192], P(('group', 'expert')), parts along dimension 0, may hold values from 1 to 64, as said below
- old_memory: bfloat16 [64, 192, 2048], P(('group', 'expert')), parts along dimension 0, may hold values from -6 to 6
- old_lengths: int32 [64], P(('group', 'expert')), parts along dimension 0, may hold values from 1 to 192, as said below
- slot_of: int32 [192], P('group'), parts along dimension 0, may hold values from 0 to 95, each once
- qkv_weight: bfloat16 [2048, 3072], P('expert'), may hold values from -0.125 to 0.125
- self_out_weight: bfloat16 [1024, 2048], P('expert'), may hold values from -0.1875 to 0.1875
- cross_query_weight: bfloat16 [2048, 1024], P('expert'), may hold values from -0.125 to 0.125
- cross_out_weight: bfloat16 [1024, 2048], P('expert'), may hold values from -0.1875 to 0.1875
Outputs:
- encoded: bfloat16 [8192, 2048], P(('group', 'expert')), parts along dimension 0
- decoded: bfloat16 [2, 192, 2048], P(None, ('group', 'expert')), parts along dimension 1
There are 2 independent parts, one for each index of `group`. A program takes and returns all parts, laid end to end along the dimension named above; an argument that names none is the same for every part. Nothing has to cross between parts.
Inputs may be any that keep to these rules, and one draw needn't show every extreme that they name: `routes`: within the rows of any device no expert is named more than 192 times, and on some device some expert reaches 192; a row names two different experts. `source_lengths`: each row sums to 256 and its largest entry is exactly 192. `context_lengths`: some slot holds exactly 64. `old_lengths`: some running request reaches 192. `slot_of`: each slot once.
All inputs are finite; a program needn't handle non-finite values.
Results may differ from a plain program's by a relative error of at most 0.0039.
Values may be sent and summed in bfloat16 or wider, within the bound.
No kernel may reach another device: no remote copies, remote signals or barrier semaphores. Data moves between devices by JAX's collectives and lax.ppermute only.
A program may use at most 128 MiB of HBM per device.

v0:
```python
import jax
import jax.numpy as jnp
from jax import lax
from jax.sharding import PartitionSpec as P

HEADS = 8
HD = 128
EXP_SPLIT = 4
SRC_DEV = 4
OLD_DEV = 2
TOK_DEV = 256
CTX = 64
KV = 1024
SRC_MAX = 192
HELD = 6


def normalized(values):
    values = values.astype(jnp.float32)
    average = jnp.mean(values, axis=-1, keepdims=True)
    centred = values - average
    variance = jnp.mean(centred * centred, axis=-1, keepdims=True)
    return centred * lax.rsqrt(variance + 1e-05)


def attend_shared(queries, all_keys, all_values, key_mask):
    scores = jnp.einsum(
        "phd,jhd->phj", queries, all_keys, preferred_element_type=jnp.float32
    ) * HD ** (-0.5)
    raised = jnp.exp(scores) * key_mask[:, None, :]
    weights_bf = (raised / jnp.sum(raised, axis=-1, keepdims=True)).astype(jnp.bfloat16)
    result = jnp.einsum("phj,jhd->phd", weights_bf, all_values, preferred_element_type=jnp.float32)
    return result.astype(jnp.bfloat16)


def expert_work(received, expert_in, expert_out):
    activated = jnp.einsum(
        "icd,df->icf", received, expert_in[0], preferred_element_type=jnp.float32
    )
    activated = jnp.maximum(activated, 0.0).astype(jnp.bfloat16)
    result = jnp.einsum("icf,fd->icd", activated, expert_out[0], preferred_element_type=jnp.float32)
    return result.astype(jnp.bfloat16)


def project(local_rows, weight, row_order):
    spread = lax.all_to_all(local_rows, "expert", split_axis=1, concat_axis=0, tiled=True)
    return lax.psum_scatter(
        jnp.dot(spread[row_order], weight, preferred_element_type=jnp.float32),
        "expert",
        scatter_dimension=0,
        tiled=True,
    )


def body(
    source_tokens,
    routes,
    source_lengths,
    router_weight,
    expert_in,
    expert_out,
    memory_weight,
    decode_inputs,
    self_cache,
    context_lengths,
    old_memory,
    old_lengths,
    slot_of,
    qkv_weight,
    self_out_weight,
    cross_query_weight,
    cross_out_weight,
):
    devices = lax.axis_size("expert")
    own_index = lax.axis_index("expert")
    token_count = source_tokens.shape[0]
    model_width = source_tokens.shape[1]
    expert_count = router_weight.shape[1]
    capacity = 3 * token_count // expert_count
    hidden_rows = normalized(source_tokens).astype(jnp.bfloat16)
    logits = jnp.dot(hidden_rows, router_weight, preferred_element_type=jnp.float32)
    one_hot = routes[:, :, None] == jnp.arange(expert_count, dtype=jnp.int32)[None, None, :]
    chosen = jnp.sum(jnp.where(one_hot, logits[:, None, :], 0.0), axis=-1)
    leading = jax.nn.sigmoid(chosen[:, 0] - chosen[:, 1])
    gate_values = jnp.stack([leading, 1.0 - leading], axis=1)
    flat_hot = one_hot.reshape(token_count * 2, expert_count).astype(jnp.int32)
    position = jnp.sum((jnp.cumsum(flat_hot, axis=0) - 1) * flat_hot, axis=-1)
    slot_index = routes.reshape(-1) * capacity + position
    repeated = jnp.broadcast_to(hidden_rows[:, None, :], (token_count, 2, model_width)).reshape(
        token_count * 2, model_width
    )
    buffer = (
        jnp.zeros((expert_count * capacity, model_width), jnp.bfloat16).at[slot_index].set(repeated)
    )
    outgoing = jnp.repeat(buffer.reshape(expert_count, capacity, model_width), EXP_SPLIT, axis=0)
    partial_value = expert_work(
        lax.all_to_all(outgoing, "expert", split_axis=0, concat_axis=0, tiled=True),
        expert_in,
        expert_out,
    )
    returned = lax.all_to_all(partial_value, "expert", split_axis=0, concat_axis=0, tiled=True)
    combined = jnp.sum(
        returned.reshape(expert_count, EXP_SPLIT, capacity, model_width).astype(jnp.float32), axis=1
    )
    gathered = combined.reshape(expert_count * capacity, model_width)[slot_index].reshape(
        token_count, 2, model_width
    )
    expert_sum = jnp.sum(gate_values[:, :, None] * gathered, axis=1)
    encoder_sum = source_tokens.astype(jnp.float32) + expert_sum
    encoded = encoder_sum.astype(jnp.bfloat16)
    memory = normalized(encoder_sum).astype(jnp.bfloat16)
    memory_kv = jnp.dot(memory, memory_weight, preferred_element_type=jnp.float32).astype(
        jnp.bfloat16
    )
    qkv_use, self_use, query_use, cross_use = (
        qkv_weight,
        self_out_weight,
        cross_query_weight,
        cross_out_weight,
    )
    slot_count = decode_inputs.shape[1]
    new_keys = memory_kv[:, :KV].reshape(TOK_DEV, HEADS, HD)
    new_values = memory_kv[:, KV:].reshape(TOK_DEV, HEADS, HD)
    bounds = jnp.cumsum(source_lengths[0])
    segment = jnp.sum(
        (jnp.arange(TOK_DEV, dtype=jnp.int32)[:, None] >= bounds[None, :]).astype(jnp.int32),
        axis=-1,
    )
    new_mask = (segment[None, :] == jnp.arange(SRC_DEV, dtype=jnp.int32)[:, None]).astype(
        jnp.float32
    )
    old_keys = old_memory[:, :, :KV].reshape(OLD_DEV, SRC_MAX, HEADS, HD)
    old_values = old_memory[:, :, KV:].reshape(OLD_DEV, SRC_MAX, HEADS, HD)
    old_mask = (jnp.arange(SRC_MAX, dtype=jnp.int32)[None, :] < old_lengths[:, None]).astype(
        jnp.float32
    )[:, None, :]
    global_slots = own_index * slot_count + jnp.arange(slot_count, dtype=jnp.int32)
    new_slots = slot_of.reshape(devices, HELD)[:, :SRC_DEV].reshape(-1)
    fresh_slot = jnp.any(global_slots[:, None] == new_slots[None, :], axis=-1)
    effective = jnp.where(fresh_slot, 0, context_lengths)
    cache_mask = (jnp.arange(CTX, dtype=jnp.int32)[None, :] < effective[:, None]).astype(
        jnp.float32
    )
    cache_keys = self_cache[:, :, :KV].reshape(slot_count, CTX, HEADS, HD)
    cache_values = self_cache[:, :, KV:].reshape(slot_count, CTX, HEADS, HD)
    inverse = jnp.zeros_like(slot_of).at[slot_of].set(jnp.arange(slot_of.shape[0], dtype=jnp.int32))
    same_rows = jnp.arange(devices * slot_count, dtype=jnp.int32)
    normed_inputs = normalized(decode_inputs).astype(jnp.bfloat16)
    new_key_list = []
    new_value_list = []
    outputs = []
    for step_index in range(2):
        current = (
            project(normed_inputs[step_index], qkv_use, same_rows)
            .astype(jnp.bfloat16)
            .reshape(slot_count, 3, HEADS, HD)
        )
        new_key_list.append(current[:, 1])
        new_value_list.append(current[:, 2])
        all_keys = jnp.concatenate([cache_keys, jnp.stack(new_key_list, axis=1)], axis=1)
        all_values = jnp.concatenate([cache_values, jnp.stack(new_value_list, axis=1)], axis=1)
        key_mask = jnp.concatenate(
            [cache_mask, jnp.ones((slot_count, step_index + 1), jnp.float32)], axis=1
        )
        attended = jax.vmap(attend_shared)(
            current[:, 0][:, None], all_keys, all_values, key_mask[:, None, :]
        ).reshape(slot_count, KV)
        after_self = decode_inputs[step_index].astype(jnp.float32) + project(
            attended, self_use, same_rows
        )
        normed_self = normalized(after_self).astype(jnp.bfloat16)
        cross_rows = (
            project(normed_self, query_use, slot_of).astype(jnp.bfloat16).reshape(HELD, HEADS, HD)
        )
        new_out = attend_shared(cross_rows[:SRC_DEV], new_keys, new_values, new_mask)
        old_out = jax.vmap(attend_shared)(
            cross_rows[SRC_DEV:][:, None], old_keys, old_values, old_mask
        )[:, 0]
        held_out = jnp.concatenate([new_out, old_out], axis=0).reshape(HELD, KV)
        cross_sum = project(held_out, cross_use, inverse)
        outputs.append((after_self + cross_sum).astype(jnp.bfloat16))
    return (encoded, jnp.stack(outputs))


def solution(mesh):
    return jax.shard_map(
        body,
        mesh=mesh,
        in_specs=(
            P(("group", "expert"), None),
            P(("group", "expert"), None),
            P(("group", "expert"), None),
            P(),
            P("expert", None, None),
            P("expert", None, None),
            P(),
            P(None, ("group", "expert"), None),
            P(("group", "expert"), None, None),
            P(("group", "expert")),
            P(("group", "expert"), None, None),
            P(("group", "expert")),
            P("group"),
            P("expert", None),
            P("expert", None),
            P("expert", None),
            P("expert", None),
        ),
        out_specs=(P(("group", "expert"), None), P(None, ("group", "expert"), None)),
        check_vma=False,
    )
```

profile of v0, /device:TPU:0, one launch (start us, length us, event | category | flops | bytes accessed | tf_op | source)
XLA Modules:
  0.0 997.0 jit_solution(16759693772423412490)
XLA Ops:
  4.5 7.4 all-to-all-start.6
  20.8 6.0 all-to-all-start.2
  26.9 6.6 all-to-all-done.2
  37.5 39.8 %fusion.134 = (f32[8,3072]{1,0:T(8,128)S(1)}, f32[8,3072]{1,0:T(8,128)S(1)}) fusion(f32[96,3072]{1,0:T(8,128)} %fusion.148, f32[96,3072]{1,0:T(8,128)} %fusion.144), kind=kCustom, calls=%all-reduce-scatter.11 | all-reduce-scatter fusion | flops 786433 | bytes 2556416
  131.3 5.7 all-to-all-done.3
  139.2 37.5 %fusion.133 = (f32[8,2048]{1,0:T(8,128)S(1)}, f32[8,2048]{1,0:T(8,128)S(1)}) fusion(f32[96,2048]{1,0:T(8,128)} %fusion.149, f32[96,2048]{1,0:T(8,128)S(1)} %fusion.145), kind=kCustom, calls=%all-reduce-scatter.10 | all-reduce-scatter fusion | flops 524289 | bytes 1704448
  210.4 6.7 scatter_custom_fusion
  217.1 8.1 broadcast_in_dim.29
  225.2 6.1 all-to-all-start
  232.3 222.8 %all-to-all-done = bf16[16,192,2048]{2,1,0:T(8,128)(2,1)} async-done(((bf16[16,192,2048]{2,1,0:T(8,128)(2,1)}), bf16[16,192,2048]{2,1,0:T(8,128)(2,1)}, u32[]{:S(2)}, u32[]{:S(2)}) %all-to-all-start) | async-done | bytes 12582944 | tf_op jit(solution)/shard_map/all_to_all | solution.py:97
  455.1 53.6 %all-to-all-start.8 = ((bf16[6,16,128]{2,0,1:T(8,128)(2,1)}), bf16[6,16,128]{2,0,1:T(8,128)(2,1)S(1)}, u32[]{:S(2)}, u32[]{:S(2)}) async-start(bf16[6,16,128]{2,0,1:T(8,128)(2,1)} %fusion.85), calls=%async_computation.8 | async-start | bytes 65536 | tf_op jit(solution)/shard_map/all_to_all | solution.py:46
  508.7 33.2 %convolution_convert_fusion = bf16[16,192,2048]{2,1,0:T(8,128)(2,1)} fusion(bf16[1,1024,2048]{2,1,0:T(8,128)(2,1)} %param.22, bf16[16,192,2048]{2,1,0:T(8,128)(2,1)} %all-to-all-done, bf16[1,2048,1024]{2,1,0:T(8,128)(2,1)} %param.21), kind=kOutput, calls=%fused_computation.17 | convolution fusion | flops 25782386688 | bytes 33554432 | tf_op jit(solution)/shard_map/icf,fd->icd/dot_general | solution.py:41
  541.9 6.3 all-to-all-start.1
  554.1 250.9 %fusion.132 = (f32[8,1024]{1,0:T(8,128)S(1)}, f32[8,1024]{1,0:T(8,128)S(1)}) fusion(f32[96,1024]{1,0:T(8,128)S(1)} %fusion.150, f32[96,1024]{1,0:T(8,128)S(1)} %fusion.146), kind=kCustom, calls=%all-reduce-scatter.9 | all-reduce-scatter fusion | flops 262145 | bytes 852480
  805.1 35.4 %collective-permute-start.9 = (bf16[8,1024]{1,0:T(8,128)(2,1)S(1)}, bf16[8,1024]{1,0:T(8,128)(2,1)S(1)}, u32[]{:S(2)}, u32[]{:S(2)}) collective-permute-start(bf16[8,1024]{1,0:T(8,128)(2,1)S(1)} %convert.46), channel_id=1, source_target_pairs={{0,2},{1,3},{2,4},{3,5},{4,6},{5,7},{6,8},{7,9},{8,10},{9,11},{10,... | collective-permute-start | bytes 49160
  840.5 7.2 collective-permute-start.10
  870.8 11.1 %convert_reduce_fusion = f32[4,192,2048]{2,1,0:T(8,128)} fusion(bf16[16,192,2048]{2,1,0:T(8,128)(2,1)} %all-to-all-done.1), kind=kLoop, calls=%fused_computation.15 | loop fusion | flops 11010048 | bytes 18874368 | tf_op jit(solution)/shard_map/reduce_sum | solution.py:102
  881.8 8.2 gather_fusion
  890.0 6.0 reshape.385
  896.0 8.9 multiply_reduce_fusion
  906.6 5.8 convolution_convert_fusion.1
  919.7 5.8 all-to-all-done.5
  929.1 6.3 all-to-all-done.9
  937.4 37.1 %fusion.131 = (f32[8,2048]{1,0:T(8,128)S(1)}, f32[8,2048]{1,0:T(8,128)S(1)}) fusion(f32[96,2048]{1,0:T(8,128)S(1)} %fusion.151, f32[96,2048]{1,0:T(8,128)S(1)} %fusion.147), kind=kCustom, calls=%all-reduce-scatter.8 | all-reduce-scatter fusion | flops 524289 | bytes 1704448
  (294 shorter events, 171.6 us)
Async XLA Ops:
  4.5 16.3 %all-to-all-start.6 = ((bf16[6,16,128]{2,0,1:T(8,128)(2,1)}), bf16[6,16,128]{2,0,1:T(8,128)(2,1)S(1)}, u32[]{:S(2)}, u32[]{:S(2)}) async-start(bf16[6,16,128]{2,0,1:T(8,128)(2,1)} %bitcast.60), calls=%async_computation.6 | async-start | bytes 65536 | tf_op jit(solution)/shard_map/all_to_all | solution.py:46
  20.8 12.7 %all-to-all-start.2 = ((bf16[6,16,128]{2,0,1:T(8,128)(2,1)}), bf16[6,16,128]{2,0,1:T(8,128)(2,1)S(1)}, u32[]{:S(2)}, u32[]{:S(2)}) async-start(bf16[6,16,128]{2,0,1:T(8,128)(2,1)} %bitcast.59), calls=%async_computation.2 | async-start | bytes 65536 | tf_op jit(solution)/shard_map/all_to_all | solution.py:46
  77.4 22.2 %collective-permute-start.1 = (bf16[8,3072]{1,0:T(8,128)(2,1)S(1)}, bf16[8,3072]{1,0:T(8,128)(2,1)S(1)}, u32[]{:S(2)}, u32[]{:S(2)}) collective-permute-start(bf16[8,3072]{1,0:T(8,128)(2,1)S(1)} %convert.44), channel_id=1, source_target_pairs={{0,2},{1,3},{2,4},{3,5},{4,6},{5,7},{6,8},{7,9},{8,10},{9,11},{10,... | collective-permute-start | bytes 147464
  81.3 20.5 %collective-permute-start.2 = (bf16[8,3072]{1,0:T(8,128)(2,1)S(1)}, bf16[8,3072]{1,0:T(8,128)(2,1)S(1)}, u32[]{:S(2)}, u32[]{:S(2)}) collective-permute-start(bf16[8,3072]{1,0:T(8,128)(2,1)S(1)} %convert.44), channel_id=1, source_target_pairs={{0,3},{1,4},{2,5},{3,6},{4,7},{5,8},{6,9},{7,10},{8,11},{9,12},{10... | collective-permute-start | bytes 147464
  82.6 21.3 %collective-permute-start = (bf16[8,3072]{1,0:T(8,128)(2,1)S(1)}, bf16[8,3072]{1,0:T(8,128)(2,1)}, u32[]{:S(2)}, u32[]{:S(2)}) collective-permute-start(bf16[8,3072]{1,0:T(8,128)(2,1)S(1)} %convert.44), channel_id=1, source_target_pairs={{0,1},{1,2},{2,3},{3,4},{4,5},{5,6},{6,7},{7,8},{8,9},{9,10},{10,1... | collective-permute-start | bytes 147464
  92.5 15.3 %collective-permute-start.17 = (bf16[8,3072]{1,0:T(8,128)(2,1)}, bf16[8,3072]{1,0:T(8,128)(2,1)}, u32[]{:S(2)}, u32[]{:S(2)}) collective-permute-start(bf16[8,3072]{1,0:T(8,128)(2,1)} %convert.45), channel_id=1, source_target_pairs={{0,2},{1,3},{2,4},{3,5},{4,6},{5,7},{6,8},{7,9},{8,10},{9,11},{10,... | collective-permute-start | bytes 147464
  95.1 12.8 %collective-permute-start.18 = (bf16[8,3072]{1,0:T(8,128)(2,1)}, bf16[8,3072]{1,0:T(8,128)(2,1)}, u32[]{:S(2)}, u32[]{:S(2)}) collective-permute-start(bf16[8,3072]{1,0:T(8,128)(2,1)} %convert.45), channel_id=1, source_target_pairs={{0,3},{1,4},{2,5},{3,6},{4,7},{5,8},{6,9},{7,10},{8,11},{9,12},{10... | collective-permute-start | bytes 147464
  176.7 15.4 %collective-permute-start.22 = (f32[8,2048]{1,0:T(8,128)S(1)}, f32[8,2048]{1,0:T(8,128)S(1)}, u32[]{:S(2)}, u32[]{:S(2)}) collective-permute-start(f32[8,2048]{1,0:T(8,128)S(1)} %get-tuple-element.22), channel_id=1, source_target_pairs={{0,3},{1,4},{2,5},{3,6},{4,7},{5,8},{6,9},{7,10},{8,11},{9,12},{10... | collective-permute-start | bytes 196616
  178.0 15.4 %collective-permute-start.21 = (f32[8,2048]{1,0:T(8,128)S(1)}, f32[8,2048]{1,0:T(8,128)S(1)}, u32[]{:S(2)}, u32[]{:S(2)}) collective-permute-start(f32[8,2048]{1,0:T(8,128)S(1)} %get-tuple-element.22), channel_id=1, source_target_pairs={{0,2},{1,3},{2,4},{3,5},{4,6},{5,7},{6,8},{7,9},{8,10},{9,11},{10,... | collective-permute-start | bytes 196616
  180.8 15.5 %collective-permute-start.20 = (f32[8,2048]{1,0:T(8,128)S(1)}, f32[8,2048]{1,0:T(8,128)S(1)}, u32[]{:S(2)}, u32[]{:S(2)}) collective-permute-start(f32[8,2048]{1,0:T(8,128)S(1)} %get-tuple-element.22), channel_id=1, source_target_pairs={{0,1},{1,2},{2,3},{3,4},{4,5},{5,6},{6,7},{7,8},{8,9},{9,10},{10,1... | collective-permute-start | bytes 196616
  182.1 15.8 %collective-permute-start.6 = (f32[8,2048]{1,0:T(8,128)S(1)}, f32[8,2048]{1,0:T(8,128)S(1)}, u32[]{:S(2)}, u32[]{:S(2)}) collective-permute-start(f32[8,2048]{1,0:T(8,128)S(1)} %get-tuple-element.23), channel_id=1, source_target_pairs={{0,3},{1,4},{2,5},{3,6},{4,7},{5,8},{6,9},{7,10},{8,11},{9,12},{10... | collective-permute-start | bytes 196616
  199.5 17.5 %all-to-all-start.4 = ((bf16[6,16,128]{2,0,1:T(8,128)(2,1)}), bf16[6,16,128]{2,0,1:T(8,128)(2,1)S(1)}, u32[]{:S(2)}, u32[]{:S(2)}) async-start(bf16[6,16,128]{2,0,1:T(8,128)(2,1)} %fusion.84), calls=%async_computation.4 | async-start | bytes 65536 | tf_op jit(solution)/shard_map/all_to_all | solution.py:46
  225.2 229.9 %all-to-all-start = ((bf16[16,192,2048]{2,1,0:T(8,128)(2,1)}), bf16[16,192,2048]{2,1,0:T(8,128)(2,1)}, u32[]{:S(2)}, u32[]{:S(2)}) async-start(bf16[16,192,2048]{2,1,0:T(8,128)(2,1)} %bitcast.247), calls=%async_computation | async-start | bytes 25165824 | tf_op jit(solution)/shard_map/all_to_all | solution.py:97
  455.1 86.8 %all-to-all-start.8 = ((bf16[6,16,128]{2,0,1:T(8,128)(2,1)}), bf16[6,16,128]{2,0,1:T(8,128)(2,1)S(1)}, u32[]{:S(2)}, u32[]{:S(2)}) async-start(bf16[6,16,128]{2,0,1:T(8,128)(2,1)} %fusion.85), calls=%async_computation.8 | async-start | bytes 65536 | tf_op jit(solution)/shard_map/all_to_all | solution.py:46
  541.9 328.9 %all-to-all-start.1 = ((bf16[16,192,2048]{2,1,0:T(8,128)(2,1)}), bf16[16,192,2048]{2,1,0:T(8,128)(2,1)}, u32[]{:S(2)}, u32[]{:S(2)}) async-start(bf16[16,192,2048]{2,1,0:T(8,128)(2,1)} %convolution_convert_fusion), calls=%async_computation.1 | async-start | bytes 25165824 | tf_op jit(solution)/shard_map/all_to_all | solution.py:101
  805.1 57.0 %collective-permute-start.9 = (bf16[8,1024]{1,0:T(8,128)(2,1)S(1)}, bf16[8,1024]{1,0:T(8,128)(2,1)S(1)}, u32[]{:S(2)}, u32[]{:S(2)}) collective-permute-start(bf16[8,1024]{1,0:T(8,128)(2,1)S(1)} %convert.46), channel_id=1, source_target_pairs={{0,2},{1,3},{2,4},{3,5},{4,6},{5,7},{6,8},{7,9},{8,10},{9,11},{10,... | collective-permute-start | bytes 49160
  840.5 22.9 %collective-permute-start.10 = (bf16[8,1024]{1,0:T(8,128)(2,1)S(1)}, bf16[8,1024]{1,0:T(8,128)(2,1)S(1)}, u32[]{:S(2)}, u32[]{:S(2)}) collective-permute-start(bf16[8,1024]{1,0:T(8,128)(2,1)S(1)} %convert.46), channel_id=1, source_target_pairs={{0,3},{1,4},{2,5},{3,6},{4,7},{5,8},{6,9},{7,10},{8,11},{9,12},{10... | collective-permute-start | bytes 49160
  847.8 18.3 %collective-permute-start.8 = (bf16[8,1024]{1,0:T(8,128)(2,1)S(1)}, bf16[8,1024]{1,0:T(8,128)(2,1)S(1)}, u32[]{:S(2)}, u32[]{:S(2)}) collective-permute-start(bf16[8,1024]{1,0:T(8,128)(2,1)S(1)} %convert.46), channel_id=1, source_target_pairs={{0,1},{1,2},{2,3},{3,4},{4,5},{5,6},{6,7},{7,8},{8,9},{9,10},{10,1... | collective-permute-start | bytes 49160
  856.0 11.0 %collective-permute-start.25 = (bf16[8,1024]{1,0:T(8,128)(2,1)S(1)}, bf16[8,1024]{1,0:T(8,128)(2,1)S(1)}, u32[]{:S(2)}, u32[]{:S(2)}) collective-permute-start(bf16[8,1024]{1,0:T(8,128)(2,1)S(1)} %convert.47), channel_id=1, source_target_pairs={{0,2},{1,3},{2,4},{3,5},{4,6},{5,7},{6,8},{7,9},{8,10},{9,11},{10,... | collective-permute-start | bytes 49160
  914.5 11.0 %all-to-all-start.5 = ((bf16[16,2,192]{2,1,0:T(2,128)(2,1)}), bf16[16,2,192]{2,1,0:T(2,128)(2,1)S(1)}, u32[]{:S(2)}, u32[]{:S(2)}) async-start(bf16[16,2,192]{2,1,0:T(2,128)(2,1)} %reshape.540), calls=%async_computation.5 | async-start | bytes 32768 | tf_op jit(solution)/shard_map/all_to_all | solution.py:46
  974.5 15.0 %collective-permute-start.30 = (f32[8,2048]{1,0:T(8,128)S(1)}, f32[8,2048]{1,0:T(8,128)S(1)}, u32[]{:S(2)}, u32[]{:S(2)}) collective-permute-start(f32[8,2048]{1,0:T(8,128)S(1)} %get-tuple-element.14), channel_id=1, source_target_pairs={{0,3},{1,4},{2,5},{3,6},{4,7},{5,8},{6,9},{7,10},{8,11},{9,12},{10... | collective-permute-start | bytes 196616
  975.8 15.0 %collective-permute-start.29 = (f32[8,2048]{1,0:T(8,128)S(1)}, f32[8,2048]{1,0:T(8,128)S(1)}, u32[]{:S(2)}, u32[]{:S(2)}) collective-permute-start(f32[8,2048]{1,0:T(8,128)S(1)} %get-tuple-element.14), channel_id=1, source_target_pairs={{0,2},{1,3},{2,4},{3,5},{4,6},{5,7},{6,8},{7,9},{8,10},{9,11},{10,... | collective-permute-start | bytes 196616
  977.1 16.5 %collective-permute-start.28 = (f32[8,2048]{1,0:T(8,128)S(1)}, f32[8,2048]{1,0:T(8,128)S(1)}, u32[]{:S(2)}, u32[]{:S(2)}) collective-permute-start(f32[8,2048]{1,0:T(8,128)S(1)} %get-tuple-element.14), channel_id=1, source_target_pairs={{0,1},{1,2},{2,3},{3,4},{4,5},{5,6},{6,7},{7,8},{8,9},{9,10},{10,1... | collective-permute-start | bytes 196616
  979.7 15.8 %collective-permute-start.14 = (f32[8,2048]{1,0:T(8,128)S(1)}, f32[8,2048]{1,0:T(8,128)S(1)}, u32[]{:S(2)}, u32[]{:S(2)}) collective-permute-start(f32[8,2048]{1,0:T(8,128)S(1)} %get-tuple-element.15), channel_id=1, source_target_pairs={{0,3},{1,4},{2,5},{3,6},{4,7},{5,8},{6,9},{7,10},{8,11},{9,12},{10... | collective-permute-start | bytes 196616
  (38 other events, 512.8 us)
where the time goes:
time: 1010 us; the launch traced here: 997 us
  blocking collectives  365 us (36%)
  waiting for transfers between devices  252 us (25%)
  starting transfers between devices  219 us (22%)
  local copies, waits for them, and re-layouts  69.9 us (7%)
  matrix products  52.1 us (5%)
  other arithmetic  35.6 us (4%)
    unnamed x4, blocking collectives  365 us
    all_to_all x1, waiting for transfers between devices, body(): lax.all_to_all(outgoing, 'expert', split_axis=0, concat_axis=0, tiled=True)  223 us
    unnamed x32, starting transfers between devices  120 us
    all_to_all x8, starting transfers between devices, project(): lax.all_to_all(local_rows, 'expert', split_axis=1, concat_axis=0, tiled=T...  86.2 us
    dot_general x1, matrix products, expert_work(): jnp.einsum('icf,fd->icd', activated, expert_out[0], preferred_element_typ...  33.2 us
    all_to_all x8, waiting for transfers between devices, project(): lax.all_to_all(local_rows, 'expert', split_axis=1, concat_axis=0, tiled=T...  26.7 us
    unnamed x75, local copies, waits for them, and re-layouts  20.9 us
  transfers between devices with their start and end apart: 42, of which 9 were waited for; matrix products, arithmetic and copies ran while one was open for 33% of the time, Pallas kernels for 0%

commit v1 on v0

v1 whole, which is shorter than its diff:
```python
import jax
import jax.numpy as jnp
from jax import lax
from jax.sharding import PartitionSpec as P

HEADS = 8
HD = 128
EXP_SPLIT = 4
SRC_DEV = 4
OLD_DEV = 2
TOK_DEV = 256
CTX = 64
KV = 1024
SRC_MAX = 192
HELD = 6
STEPS = 2
BF = jnp.bfloat16
F32 = jnp.float32


def normalized(values):
    values = values.astype(jnp.float32)
    average = jnp.mean(values, axis=-1, keepdims=True)
    centred = values - average
    variance = jnp.mean(centred * centred, axis=-1, keepdims=True)
    return centred * lax.rsqrt(variance + 1e-05)


def attend_shared(queries, all_keys, all_values, key_mask):
    scores = jnp.einsum("phd,jhd->phj", queries, all_keys, preferred_element_type=F32) * HD ** (-0.5)
    raised = jnp.exp(scores) * key_mask[:, None, :]
    weights_bf = (raised / jnp.sum(raised, axis=-1, keepdims=True)).astype(BF)
    result = jnp.einsum("phj,jhd->phd", weights_bf, all_values, preferred_element_type=F32)
    return result.astype(BF)


def swap(values, devices, bit):
    return lax.ppermute(values, "expert", [(i, i ^ bit) for i in range(devices)])


def turn(values, devices, distance):
    step = EXP_SPLIT * distance
    return lax.ppermute(values, "expert", [(i, (i + step) % devices) for i in range(devices)])


def turn_order(planes):
    order = []
    for distance in range(1, planes // 2 + 1):
        order.append(distance)
        if planes - distance != distance:
            order.append(planes - distance)
    return order


def summed_rows(partial, devices, own_index):
    planes = devices // EXP_SPLIT
    rows = partial.shape[0] // devices
    blocks = partial.reshape(planes, 2, 2, rows, partial.shape[1])
    core = own_index % 2
    side = (own_index // 2) % 2
    plane = own_index // EXP_SPLIT
    kept = jnp.where(core == 0, blocks[:, :, 0], blocks[:, :, 1])
    sent = jnp.where(core == 0, blocks[:, :, 1], blocks[:, :, 0]).astype(BF)
    kept = kept + swap(sent, devices, 1).astype(F32)
    sent = jnp.where(side == 0, kept[:, 1], kept[:, 0]).astype(BF)
    kept = jnp.where(side == 0, kept[:, 0], kept[:, 1]) + swap(sent, devices, 2).astype(F32)
    total = lax.dynamic_index_in_dim(kept, plane, 0, keepdims=False)
    low = kept.astype(BF)
    for distance in turn_order(planes):
        block = lax.dynamic_index_in_dim(low, (plane + distance) % planes, 0, keepdims=False)
        total = total + turn(block, devices, distance).astype(F32)
    return total


def project(local_rows, weight, order, devices, own_index):
    spread = lax.all_to_all(local_rows, "expert", split_axis=1, concat_axis=0, tiled=True)
    if order is not None:
        spread = jnp.dot(order, spread, preferred_element_type=F32).astype(BF)
    return summed_rows(jnp.dot(spread, weight, preferred_element_type=F32), devices, own_index)


def body(
    source_tokens,
    routes,
    source_lengths,
    router_weight,
    expert_in,
    expert_out,
    memory_weight,
    decode_inputs,
    self_cache,
    context_lengths,
    old_memory,
    old_lengths,
    slot_of,
    qkv_weight,
    self_out_weight,
    cross_query_weight,
    cross_out_weight,
):
    devices = lax.axis_size("expert")
    own_index = lax.axis_index("expert")
    token_count = source_tokens.shape[0]
    expert_count = router_weight.shape[1]
    planes = devices // EXP_SPLIT
    plane = own_index // EXP_SPLIT
    capacity = 3 * token_count // expert_count
    slot_count = decode_inputs.shape[1]

    hidden_rows = normalized(source_tokens).astype(BF)
    logits = jnp.dot(hidden_rows, router_weight, preferred_element_type=F32)
    one_hot = routes[:, :, None] == jnp.arange(expert_count, dtype=jnp.int32)[None, None, :]
    chosen = jnp.sum(jnp.where(one_hot, logits[:, None, :], 0.0), axis=-1)
    leading = jax.nn.sigmoid(chosen[:, 0] - chosen[:, 1])
    member = jnp.any(one_hot, axis=1)
    earlier = (
        jnp.arange(token_count, dtype=jnp.int32)[:, None] > jnp.arange(token_count, dtype=jnp.int32)[None, :]
    ).astype(BF)
    rank = jnp.dot(earlier, member.astype(BF), preferred_element_type=F32).astype(jnp.int32)
    w_in = expert_in[0]
    w_out = expert_out[0]

    def choice(distance):
        target = (plane + distance) % planes
        is_target = jnp.arange(expert_count, dtype=jnp.int32) == target
        there = jnp.any(member & is_target[None, :], axis=1)
        place = jnp.sum(jnp.where(is_target[None, :], rank, 0), axis=1)
        place = jnp.where(there, place, -1)
        gate = jnp.where(routes[:, 0] == target, leading, 0.0) + jnp.where(
            routes[:, 1] == target, 1.0 - leading, 0.0
        )
        return place, gate

    distances = turn_order(planes) + [0]
    spots = jnp.arange(capacity, dtype=jnp.int32)
    choices = {d: choice(d) for d in distances}

    def picked(distance):
        place, _ = choices[distance]
        pick = (place[None, :] == spots[:, None]).astype(BF)
        return jnp.dot(pick, hidden_rows, preferred_element_type=F32).astype(BF)

    back = {}
    for distance in [0] + turn_order(planes):
        block = picked(distance)
        if distance:
            block = turn(block, devices, distance)
        other_side = swap(block, devices, 2)
        other_core = swap(block, devices, 1)
        diagonal = swap(other_side, devices, 1)
        rows = jnp.concatenate([block, other_side, other_core, diagonal], axis=0)
        active = jnp.maximum(jnp.dot(rows, w_in, preferred_element_type=F32), 0.0).astype(BF)
        partial = jnp.dot(active, w_out, preferred_element_type=F32)
        half = partial[: 2 * capacity] + swap(partial[2 * capacity :].astype(BF), devices, 1).astype(F32)
        full = half[:capacity] + swap(half[capacity:].astype(BF), devices, 2).astype(F32)
        full = full.astype(BF)
        back[distance] = turn(full, devices, planes - distance) if distance else full

    global_slots = own_index * slot_count + jnp.arange(slot_count, dtype=jnp.int32)
    new_slots = slot_of.reshape(devices, HELD)[:, :SRC_DEV].reshape(-1)
    fresh_slot = jnp.any(global_slots[:, None] == new_slots[None, :], axis=-1)
    effective = jnp.where(fresh_slot, 0, context_lengths)
    cache_mask = (jnp.arange(CTX, dtype=jnp.int32)[None, :] < effective[:, None]).astype(F32)
    cache_keys = self_cache[:, :, :KV].reshape(slot_count, CTX, HEADS, HD)
    cache_values = self_cache[:, :, KV:].reshape(slot_count, CTX, HEADS, HD)
    count = slot_of.shape[0]
    to_request = (slot_of[:, None] == jnp.arange(count, dtype=jnp.int32)[None, :]).astype(BF)

    def spread_order(matrix):
        by_device = matrix.reshape(devices, HELD, devices, HELD)
        full = by_device[:, None, :, :, None, :] * jnp.eye(STEPS, dtype=BF)[None, :, None, None, :, None]
        return full.reshape(STEPS * count, STEPS * count)

    order_request = spread_order(to_request)
    order_slot = spread_order(to_request.T)

    normed_inputs = normalized(decode_inputs).astype(BF).reshape(STEPS * slot_count, -1)
    current = project(normed_inputs, qkv_weight, None, devices, own_index).astype(BF)
    current = current.reshape(STEPS, slot_count, 3, HEADS, HD).transpose(1, 0, 2, 3, 4)
    all_keys = jnp.concatenate([cache_keys, current[:, :, 1]], axis=1)
    all_values = jnp.concatenate([cache_values, current[:, :, 2]], axis=1)
    steps = jnp.arange(STEPS, dtype=jnp.int32)
    causal = (steps[:, None] >= steps[None, :]).astype(F32)
    key_mask = jnp.concatenate(
        [
            jnp.broadcast_to(cache_mask[:, None, :], (slot_count, STEPS, CTX)),
            jnp.broadcast_to(causal[None], (slot_count, STEPS, STEPS)),
        ],
        axis=2,
    )
    attended = jax.vmap(attend_shared)(current[:, :, 0], all_keys, all_values, key_mask)
    attended = attended.transpose(1, 0, 2, 3).reshape(STEPS * slot_count, KV)
    after_self = decode_inputs.astype(F32).reshape(STEPS * slot_count, -1) + project(
        attended, self_out_weight, None, devices, own_index
    )
    normed_self = normalized(after_self).astype(BF)
    cross_rows = project(normed_self, cross_query_weight, order_request, devices, own_index).astype(BF)
    cross_rows = cross_rows.reshape(STEPS, HELD, HEADS, HD)
    old_keys = old_memory[:, :, :KV].reshape(OLD_DEV, SRC_MAX, HEADS, HD)
    old_values = old_memory[:, :, KV:].reshape(OLD_DEV, SRC_MAX, HEADS, HD)
    old_mask = (jnp.arange(SRC_MAX, dtype=jnp.int32)[None, :] < old_lengths[:, None]).astype(F32)
    old_out = jax.vmap(attend_shared)(
        cross_rows[:, SRC_DEV:].transpose(1, 0, 2, 3),
        old_keys,
        old_values,
        jnp.broadcast_to(old_mask[:, None, :], (OLD_DEV, STEPS, SRC_MAX)),
    ).transpose(1, 0, 2, 3)

    encoder_sum = source_tokens.astype(F32)
    for distance in distances:
        place, gate = choices[distance]
        pick = (place[:, None] == spots[None, :]).astype(BF)
        encoder_sum = encoder_sum + gate[:, None] * jnp.dot(pick, back[distance], preferred_element_type=F32)
    encoded = encoder_sum.astype(BF)
    memory = normalized(encoder_sum).astype(BF)
    memory_kv = jnp.dot(memory, memory_weight, preferred_element_type=F32).astype(BF)
    new_keys = memory_kv[:, :KV].reshape(TOK_DEV, HEADS, HD)
    new_values = memory_kv[:, KV:].reshape(TOK_DEV, HEADS, HD)
    bounds = jnp.cumsum(source_lengths[0])
    segment = jnp.sum(
        (jnp.arange(TOK_DEV, dtype=jnp.int32)[:, None] >= bounds[None, :]).astype(jnp.int32),
        axis=-1,
    )
    new_mask = (segment[None, :] == jnp.arange(SRC_DEV, dtype=jnp.int32)[:, None]).astype(F32)
    new_out = attend_shared(
        cross_rows[:, :SRC_DEV].reshape(STEPS * SRC_DEV, HEADS, HD),
        new_keys,
        new_values,
        jnp.tile(new_mask, (STEPS, 1)),
    ).reshape(STEPS, SRC_DEV, HEADS, HD)
    held_out = jnp.concatenate([new_out, old_out], axis=1).reshape(STEPS * HELD, KV)
    cross_sum = project(held_out, cross_out_weight, order_slot, devices, own_index)
    decoded = (after_self + cross_sum).astype(BF).reshape(STEPS, slot_count, -1)
    return (encoded, decoded)


def solution(mesh):
    return jax.shard_map(
        body,
        mesh=mesh,
        in_specs=(
            P(("group", "expert"), None),
            P(("group", "expert"), None),
            P(("group", "expert"), None),
            P(),
            P("expert", None, None),
            P("expert", None, None),
            P(),
            P(None, ("group", "expert"), None),
            P(("group", "expert"), None, None),
            P(("group", "expert")),
            P(("group", "expert"), None, None),
            P(("group", "expert")),
            P("group"),
            P("expert", None),
            P("expert", None),
            P("expert", None),
            P("expert", None),
        ),
        out_specs=(P(("group", "expert"), None), P(None, ("group", "expert"), None)),
        check_vma=False,
    )
```

time: 1010 us -> 410 us (0.41); the launches traced: 997 us -> 407 us
  blocking collectives: 365 us -> 0 us
  starting transfers between devices: 219 us -> 70.6 us
  local copies, waits for them, and re-layouts: 69.9 us -> 23.7 us
  waiting for transfers between devices: 252 us -> 228 us
  other arithmetic: 35.6 us -> 25.1 us
    unnamed x4 -> x0, blocking collectives: 365 us -> none
    all_to_all x2 -> x0, waiting for transfers between devices: 223 us -> none  [the longest x1 223 us: body(): lax.all_to_all(outgoing, 'expert', split_axis=0, concat_axis=0, tiled=True)]
    ppermute x0 -> x46, waiting for transfers between devices: none -> 186 us  [the longest x28 118 us: swap(): lax.ppermute(values, 'expert', [(i, i ^ bit) for i in range(devices)])]
    unnamed x32 -> x0, starting transfers between devices: 120 us -> none
    all_to_all x8 -> x4, starting transfers between devices: 86.2 us -> 17 us  [project(): lax.all_to_all(local_rows, 'expert', split_axis=1, concat_axis=0, tiled=T...]
    ppermute x0 -> x46, starting transfers between devices: none -> 53.6 us  [the longest x18 35.4 us: turn(): lax.ppermute(values, 'expert', [(i, (i + step) % devices) for i in range(...]
    reduce_sum x3 -> x0, other arithmetic: 20 us -> none  [the longest x1 11.1 us: body(): jnp.sum(returned.reshape(expert_count, EXP_SPLIT, capacity, model_width)....]
    all_to_all x8 -> x4, waiting for transfers between devices: 26.7 us -> 41.9 us  [project(): lax.all_to_all(local_rows, 'expert', split_axis=1, concat_axis=0, tiled=T...]
  transfers between devices with their start and end apart: 42 -> 50, of which waited for: 9 -> 24; matrix products, arithmetic and copies ran while one was open for 33% -> 21% of each run, Pallas kernels for 0% -> 0%
where the time goes in v1:
time: 410 us; the launch traced here: 407 us
  waiting for transfers between devices  228 us (56%)
  starting transfers between devices  70.6 us (17%)
  matrix products  58 us (14%)
  other arithmetic  25.1 us (6%)
  local copies, waits for them, and re-layouts  23.7 us (6%)
    ppermute x28, waiting for transfers between devices, swap(): lax.ppermute(values, 'expert', [(i, i ^ bit) for i in range(devices)])  118 us
    ppermute x18, waiting for transfers between devices, turn(): lax.ppermute(values, 'expert', [(i, (i + step) % devices) for i in range(...  67.7 us
    all_to_all x4, waiting for transfers between devices, project(): lax.all_to_all(local_rows, 'expert', split_axis=1, concat_axis=0, tiled=T...  41.9 us
    ppermute x18, starting transfers between devices, turn(): lax.ppermute(values, 'expert', [(i, (i + step) % devices) for i in range(...  35.4 us
    dot_general x4, matrix products, body(): jnp.dot(rows, w_in, preferred_element_type=F32)  25.1 us
    ppermute x28, starting transfers between devices, swap(): lax.ppermute(values, 'expert', [(i, i ^ bit) for i in range(devices)])  18.3 us
    all_to_all x4, starting transfers between devices, project(): lax.all_to_all(local_rows, 'expert', split_axis=1, concat_axis=0, tiled=T...  17 us
    dot_general x4, matrix products, body(): partial = jnp.dot(active, w_out, preferred_element_type=F32)  16 us
  transfers between devices with their start and end apart: 50, of which 24 were waited for; matrix products, arithmetic and copies ran while one was open for 21% of the time, Pallas kernels for 0%

profile of v1, /device:TPU:0, one launch (start us, length us, event | category | flops | bytes accessed | tf_op | source)
XLA Modules:
  0.0 407.3 jit_solution(9781497616877600641)
XLA Ops:
  10.9 5.1 %all-to-all-start = ((bf16[12,16,128]{2,0,1:T(8,128)(2,1)}), bf16[12,16,128]{2,0,1:T(8,128)(2,1)}, u32[]{:S(2)}, u32[]{:S(2)}) async-start(bf16[12,16,128]{2,0,1:T(8,128)(2,1)} %copy.146), calls=%async_computation | async-start | bytes 131072 | tf_op jit(solution)/shard_map/all_to_all | solution.py:76
  33.3 4.9 %broadcast_multiply_fusion = (bf16[16,2,6,16,2,6]{5,4,3,2,1,0:T(2,128)(2,1)}, bf16[16,2,6,16,2,6]{5,4,3,2,1,0:T(2,128)(2,1)}) fusion(bf16[16,6,16,6]{3,2,1,0:T(8,128)(2,1)S(1)} %get-tuple-element.54, bf16[2,2]{1,0:T(2,128)(2,1)} %compare_convert_fusion.3, bf16[16,6,16,6]{3,2,1,0:T(8,128)(2,1)} %get-tuple-element.55), kind=kLoop, calls=%fused_computation.141 | loop fusion | flops 73728 | bytes 184328 | tf_op jit(solution)/shard_map/mul | solution.py:171
  41.9 9.5 %collective-permute-done.27 = bf16[4,12,3072]{2,1,0:T(8,128)(2,1)S(1)} collective-permute-done((bf16[4,12,3072]{2,1,0:T(8,128)(2,1)S(1)}, bf16[4,12,3072]{2,1,0:T(8,128)(2,1)S(1)}, u32[]{:S(2)}, u32[]{:S(2)}) %collective-permute-start.27) | collective-permute-done | bytes 294944 | tf_op jit(solution)/shard_map/ppermute | solution.py:38
  59.5 4.9 %collective-permute-done.30 = bf16[12,3072]{1,0:T(8,128)(2,1)S(1)} collective-permute-done((bf16[12,3072]{1,0:T(8,128)(2,1)S(1)}, bf16[12,3072]{1,0:T(8,128)(2,1)S(1)}, u32[]{:S(2)}, u32[]{:S(2)}) %collective-permute-start.30) | collective-permute-done | bytes 73760 | tf_op jit(solution)/shard_map/ppermute | solution.py:43
  66.4 4.2 %all-to-all-start.1 = ((bf16[16,2,384]{2,1,0:T(2,128)(2,1)}), bf16[16,2,384]{2,1,0:T(2,128)(2,1)S(1)}, u32[]{:S(2)}, u32[]{:S(2)}) async-start(bf16[16,2,384]{2,1,0:T(2,128)(2,1)} %reshape.403), calls=%async_computation.1 | async-start | bytes 49152 | tf_op jit(solution)/shard_map/all_to_all | solution.py:76
  70.7 6.5 %all-to-all-done.1 = bf16[16,2,384]{2,1,0:T(2,128)(2,1)S(1)} async-done(((bf16[16,2,384]{2,1,0:T(2,128)(2,1)}), bf16[16,2,384]{2,1,0:T(2,128)(2,1)S(1)}, u32[]{:S(2)}, u32[]{:S(2)}) %all-to-all-start.1) | async-done | bytes 24608 | tf_op jit(solution)/shard_map/all_to_all | solution.py:76
  80.6 7.9 %collective-permute-done.32 = bf16[4,12,2048]{2,1,0:T(8,128)(2,1)S(1)} collective-permute-done((bf16[4,12,2048]{2,1,0:T(8,128)(2,1)S(1)}, bf16[4,12,2048]{2,1,0:T(8,128)(2,1)S(1)}, u32[]{:S(2)}, u32[]{:S(2)}) %collective-permute-start.32) | collective-permute-done | bytes 196640 | tf_op jit(solution)/shard_map/ppermute | solution.py:38
  89.8 15.2 %collective-permute-start.34 = (bf16[12,2048]{1,0:T(8,128)(2,1)}, bf16[12,2048]{1,0:T(8,128)(2,1)}, u32[]{:S(2)}, u32[]{:S(2)}) collective-permute-start(bf16[12,2048]{1,0:T(8,128)(2,1)} %get-tuple-element.48), channel_id=1, source_target_pairs={{0,12},{1,13},{2,14},{3,15},{4,0},{5,1},{6,2},{7,3},{8,4},{9,5},{1... | collective-permute-start | bytes 147464 | tf_op jit(solution)/shard_map/ppermute | solution.py:43
  118.5 28.3 %all-to-all-done.2 = bf16[12,16,128]{2,0,1:T(8,128)(2,1)S(1)} async-done(((bf16[12,16,128]{2,0,1:T(8,128)(2,1)}), bf16[12,16,128]{2,0,1:T(8,128)(2,1)S(1)}, u32[]{:S(2)}, u32[]{:S(2)}) %all-to-all-start.2) | async-done | bytes 49184 | tf_op jit(solution)/shard_map/all_to_all | solution.py:76
  160.3 6.6 %maximum_convert_fusion = bf16[768,1024]{1,0:T(8,128)(2,1)S(1)} fusion(bf16[1,2048,1024]{2,1,0:T(8,128)(2,1)} %param.21, bf16[192,2048]{1,0:T(8,128)(2,1)} %collective-permute-done.23, bf16[192,2048]{1,0:T(8,128)(2,1)} %collective-permute-done.22, bf16[192,2048]{1,0:T(8,128)(2,1)} %collective-permute-done.21, bf16[192,2048]{1,0:T(8,128)(2,1)} %convolution_convert_fusion.1), kind=kOutput, calls=%fused_computation.52 | convolution fusion | flops 3235381248 | bytes 8912896 | tf_op jit(solution)/shard_map/dot_general | solution.py:152
  166.9 22.3 %collective-permute-done.14 = bf16[192,2048]{1,0:T(8,128)(2,1)} collective-permute-done((bf16[192,2048]{1,0:T(8,128)(2,1)}, bf16[192,2048]{1,0:T(8,128)(2,1)}, u32[]{:S(2)}, u32[]{:S(2)}) %collective-permute-start.14) | collective-permute-done | bytes 786464 | tf_op jit(solution)/shard_map/ppermute | solution.py:43
  199.6 10.5 %collective-permute-done.1 = bf16[192,2048]{1,0:T(8,128)(2,1)} collective-permute-done((bf16[192,2048]{1,0:T(8,128)(2,1)}, bf16[192,2048]{1,0:T(8,128)(2,1)}, u32[]{:S(2)}, u32[]{:S(2)}) %collective-permute-start.1) | collective-permute-done | bytes 786464 | tf_op jit(solution)/shard_map/ppermute | solution.py:38
  210.5 14.9 %collective-permute-done.15 = bf16[192,2048]{1,0:T(8,128)(2,1)} collective-permute-done((bf16[192,2048]{1,0:T(8,128)(2,1)}, bf16[192,2048]{1,0:T(8,128)(2,1)}, u32[]{:S(2)}, u32[]{:S(2)}) %collective-permute-start.15) | collective-permute-done | bytes 786464 | tf_op jit(solution)/shard_map/ppermute | solution.py:38
  226.0 6.6 %maximum_convert_fusion.2 = bf16[768,1024]{1,0:T(8,128)(2,1)S(1)} fusion(bf16[1,2048,1024]{2,1,0:T(8,128)(2,1)} %param.21, bf16[192,2048]{1,0:T(8,128)(2,1)} %collective-permute-done.10, bf16[192,2048]{1,0:T(8,128)(2,1)} %collective-permute-done.9, bf16[192,2048]{1,0:T(8,128)(2,1)} %collective-permute-done.8, bf16[192,2048]{1,0:T(8,128)(2,1)} %collective-permute-done.7), kind=kOutput, calls=%fused_computation.54 | convolution fusion | flops 3235381248 | bytes 8912896 | tf_op jit(solution)/shard_map/dot_general | solution.py:152
  236.3 5.2 %maximum_convert_fusion.1 = bf16[768,1024]{1,0:T(8,128)(2,1)S(1)} fusion(bf16[1,2048,1024]{2,1,0:T(8,128)(2,1)S(1)} %copy-done.33, bf16[192,2048]{1,0:T(8,128)(2,1)S(1)} %collective-permute-done.17, bf16[192,2048]{1,0:T(8,128)(2,1)S(1)} %collective-permute-done.16, bf16[192,2048]{1,0:T(8,128)(2,1)} %collective-permute-done.15, ...), kind=kOutput, calls=%fused_computation.53 | convolution fusion | flops 3235381248 | bytes 8912896 | tf_op jit(solution)/shard_map/dot_general | solution.py:152
  245.8 6.7 %maximum_convert_fusion.3 = bf16[768,1024]{1,0:T(8,128)(2,1)} fusion(bf16[1,2048,1024]{2,1,0:T(8,128)(2,1)S(1)} %copy-done.33, bf16[192,2048]{1,0:T(8,128)(2,1)S(1)} %collective-permute-done.3, bf16[192,2048]{1,0:T(8,128)(2,1)} %collective-permute-done.2, bf16[192,2048]{1,0:T(8,128)(2,1)} %collective-permute-done.1, bf16[192,2048]{1,0:T(8,128)(2,1)} %collective-permute-done), kind=kOutput, calls=%fused_computation.55 | convolution fusion | flops 3235381248 | bytes 8912896 | tf_op jit(solution)/shard_map/dot_general | solution.py:152
  252.6 5.7 %fusion.6 = f32[768,2048]{1,0:T(8,128)S(1)} fusion(bf16[768,1024]{1,0:T(8,128)(2,1)} %maximum_convert_fusion.3, bf16[1,1024,2048]{2,1,0:T(8,128)(2,1)} %param.22), kind=kOutput, calls=%fused_computation.6 | convolution fusion | flops 3221225472 | bytes 12058624 | tf_op jit(solution)/shard_map/dot_general | solution.py:153
  269.4 26.9 %collective-permute-done.12 = bf16[192,2048]{1,0:T(8,128)(2,1)S(1)} collective-permute-done((bf16[192,2048]{1,0:T(8,128)(2,1)S(1)}, bf16[192,2048]{1,0:T(8,128)(2,1)S(1)}, u32[]{:S(2)}, u32[]{:S(2)}) %collective-permute-start.12) | collective-permute-done | bytes 786464 | tf_op jit(solution)/shard_map/ppermute | solution.py:38
  296.7 16.5 %collective-permute-done.19 = bf16[192,2048]{1,0:T(8,128)(2,1)S(1)} collective-permute-done((bf16[192,2048]{1,0:T(8,128)(2,1)S(1)}, bf16[192,2048]{1,0:T(8,128)(2,1)S(1)}, u32[]{:S(2)}, u32[]{:S(2)}) %collective-permute-start.19) | collective-permute-done | bytes 786464 | tf_op jit(solution)/shard_map/ppermute | solution.py:38
  313.5 16.1 %collective-permute-done.5 = bf16[192,2048]{1,0:T(8,128)(2,1)S(1)} collective-permute-done((bf16[192,2048]{1,0:T(8,128)(2,1)S(1)}, bf16[192,2048]{1,0:T(8,128)(2,1)S(1)}, u32[]{:S(2)}, u32[]{:S(2)}) %collective-permute-start.5) | collective-permute-done | bytes 786464 | tf_op jit(solution)/shard_map/ppermute | solution.py:38
  333.1 17.9 %collective-permute-done.20 = bf16[192,2048]{1,0:T(8,128)(2,1)S(1)} collective-permute-done((bf16[192,2048]{1,0:T(8,128)(2,1)S(1)}, bf16[192,2048]{1,0:T(8,128)(2,1)S(1)}, u32[]{:S(2)}, u32[]{:S(2)}) %collective-permute-start.20) | collective-permute-done | bytes 786464 | tf_op jit(solution)/shard_map/ppermute | solution.py:43
  351.5 14.5 %collective-permute-done.6 = bf16[192,2048]{1,0:T(8,128)(2,1)S(1)} collective-permute-done((bf16[192,2048]{1,0:T(8,128)(2,1)S(1)}, bf16[192,2048]{1,0:T(8,128)(2,1)S(1)}, u32[]{:S(2)}, u32[]{:S(2)}) %collective-permute-start.6) | collective-permute-done | bytes 786464 | tf_op jit(solution)/shard_map/ppermute | solution.py:43
  372.3 4.0 all-to-all-start.3
  389.2 7.9 %collective-permute-done.42 = bf16[4,12,2048]{2,1,0:T(8,128)(2,1)S(1)} collective-permute-done((bf16[4,12,2048]{2,1,0:T(8,128)(2,1)S(1)}, bf16[4,12,2048]{2,1,0:T(8,128)(2,1)S(1)}, u32[]{:S(2)}, u32[]{:S(2)}) %collective-permute-start.42) | collective-permute-done | bytes 196640 | tf_op jit(solution)/shard_map/ppermute | solution.py:38
  (323 shorter events, 136.0 us)
Async XLA Ops:
  6.7 140.9 %collective-permute-start.21 = (bf16[192,2048]{1,0:T(8,128)(2,1)}, bf16[192,2048]{1,0:T(8,128)(2,1)}, u32[]{:S(2)}, u32[]{:S(2)}) collective-permute-start(bf16[192,2048]{1,0:T(8,128)(2,1)} %convolution_convert_fusion.1), channel_id=1, source_target_pairs={{0,2},{1,3},{2,0},{3,1},{4,6},{5,7},{6,4},{7,5},{8,10},{9,11},{10,... | collective-permute-start | bytes 2359304 | tf_op jit(solution)/shard_map/ppermute | solution.py:38
  9.7 146.7 %collective-permute-start.22 = (bf16[192,2048]{1,0:T(8,128)(2,1)}, bf16[192,2048]{1,0:T(8,128)(2,1)}, u32[]{:S(2)}, u32[]{:S(2)}) collective-permute-start(bf16[192,2048]{1,0:T(8,128)(2,1)} %convolution_convert_fusion.1), channel_id=1, source_target_pairs={{0,1},{1,0},{2,3},{3,2},{4,5},{5,4},{6,7},{7,6},{8,9},{9,8},{10,11... | collective-permute-start | bytes 2359304 | tf_op jit(solution)/shard_map/ppermute | solution.py:38
  108.9 58.0 %collective-permute-start = (bf16[192,2048]{1,0:T(8,128)(2,1)S(1)}, bf16[192,2048]{1,0:T(8,128)(2,1)}, u32[]{:S(2)}, u32[]{:S(2)}) collective-permute-start(bf16[192,2048]{1,0:T(8,128)(2,1)S(1)} %copy-done.13), channel_id=1, source_target_pairs={{0,4},{1,5},{2,6},{3,7},{4,8},{5,9},{6,10},{7,11},{8,12},{9,13},{1... | collective-permute-start | bytes 2359304 | tf_op jit(solution)/shard_map/ppermute | solution.py:43
  109.6 41.3 %collective-permute-start.7 = (bf16[192,2048]{1,0:T(8,128)(2,1)}, bf16[192,2048]{1,0:T(8,128)(2,1)}, u32[]{:S(2)}, u32[]{:S(2)}) collective-permute-start(bf16[192,2048]{1,0:T(8,128)(2,1)} %convolution_convert_fusion.3), channel_id=1, source_target_pairs={{0,12},{1,13},{2,14},{3,15},{4,0},{5,1},{6,2},{7,3},{8,4},{9,5},{1... | collective-permute-start | bytes 2359304 | tf_op jit(solution)/shard_map/ppermute | solution.py:43
  114.8 32.0 %all-to-all-start.2 = ((bf16[12,16,128]{2,0,1:T(8,128)(2,1)}), bf16[12,16,128]{2,0,1:T(8,128)(2,1)S(1)}, u32[]{:S(2)}, u32[]{:S(2)}) async-start(bf16[12,16,128]{2,0,1:T(8,128)(2,1)} %copy.167), calls=%async_computation.2 | async-start | bytes 131072 | tf_op jit(solution)/shard_map/all_to_all | solution.py:76
  150.8 38.4 %collective-permute-start.14 = (bf16[192,2048]{1,0:T(8,128)(2,1)}, bf16[192,2048]{1,0:T(8,128)(2,1)}, u32[]{:S(2)}, u32[]{:S(2)}) collective-permute-start(bf16[192,2048]{1,0:T(8,128)(2,1)} %convolution_convert_fusion.2), channel_id=1, source_target_pairs={{0,8},{1,9},{2,10},{3,11},{4,12},{5,13},{6,14},{7,15},{8,0},{9,1},... | collective-permute-start | bytes 2359304 | tf_op jit(solution)/shard_map/ppermute | solution.py:43
  154.7 35.0 %collective-permute-start.8 = (bf16[192,2048]{1,0:T(8,128)(2,1)}, bf16[192,2048]{1,0:T(8,128)(2,1)}, u32[]{:S(2)}, u32[]{:S(2)}) collective-permute-start(bf16[192,2048]{1,0:T(8,128)(2,1)} %collective-permute-done.7), channel_id=1, source_target_pairs={{0,2},{1,3},{2,0},{3,1},{4,6},{5,7},{6,4},{7,5},{8,10},{9,11},{10,... | collective-permute-start | bytes 2359304 | tf_op jit(solution)/shard_map/ppermute | solution.py:38
  156.4 34.9 %collective-permute-start.38 = (bf16[12,1024]{1,0:T(8,128)(2,1)S(1)}, bf16[12,1024]{1,0:T(8,128)(2,1)S(1)}, u32[]{:S(2)}, u32[]{:S(2)}) collective-permute-start(bf16[12,1024]{1,0:T(8,128)(2,1)S(1)} %get-tuple-element.49), channel_id=1, source_target_pairs={{0,4},{1,5},{2,6},{3,7},{4,8},{5,9},{6,10},{7,11},{8,12},{9,13},{1... | collective-permute-start | bytes 73736 | tf_op jit(solution)/shard_map/ppermute | solution.py:43
  157.2 34.1 %collective-permute-start.39 = (bf16[12,1024]{1,0:T(8,128)(2,1)S(1)}, bf16[12,1024]{1,0:T(8,128)(2,1)S(1)}, u32[]{:S(2)}, u32[]{:S(2)}) collective-permute-start(bf16[12,1024]{1,0:T(8,128)(2,1)S(1)} %get-tuple-element.51), channel_id=1, source_target_pairs={{0,12},{1,13},{2,14},{3,15},{4,0},{5,1},{6,2},{7,3},{8,4},{9,5},{1... | collective-permute-start | bytes 73736 | tf_op jit(solution)/shard_map/ppermute | solution.py:43
  166.8 43.2 %collective-permute-start.9 = (bf16[192,2048]{1,0:T(8,128)(2,1)}, bf16[192,2048]{1,0:T(8,128)(2,1)}, u32[]{:S(2)}, u32[]{:S(2)}) collective-permute-start(bf16[192,2048]{1,0:T(8,128)(2,1)} %collective-permute-done.7), channel_id=1, source_target_pairs={{0,1},{1,0},{2,3},{3,2},{4,5},{5,4},{6,7},{7,6},{8,9},{9,8},{10,11... | collective-permute-start | bytes 2359304 | tf_op jit(solution)/shard_map/ppermute | solution.py:38
  189.3 20.8 %collective-permute-start.1 = (bf16[192,2048]{1,0:T(8,128)(2,1)}, bf16[192,2048]{1,0:T(8,128)(2,1)}, u32[]{:S(2)}, u32[]{:S(2)}) collective-permute-start(bf16[192,2048]{1,0:T(8,128)(2,1)} %collective-permute-done), channel_id=1, source_target_pairs={{0,2},{1,3},{2,0},{3,1},{4,6},{5,7},{6,4},{7,5},{8,10},{9,11},{10,... | collective-permute-start | bytes 2359304 | tf_op jit(solution)/shard_map/ppermute | solution.py:38
  189.7 35.7 %collective-permute-start.15 = (bf16[192,2048]{1,0:T(8,128)(2,1)}, bf16[192,2048]{1,0:T(8,128)(2,1)}, u32[]{:S(2)}, u32[]{:S(2)}) collective-permute-start(bf16[192,2048]{1,0:T(8,128)(2,1)} %collective-permute-done.14), channel_id=1, source_target_pairs={{0,2},{1,3},{2,0},{3,1},{4,6},{5,7},{6,4},{7,5},{8,10},{9,11},{10,... | collective-permute-start | bytes 2359304 | tf_op jit(solution)/shard_map/ppermute | solution.py:38
  191.3 34.2 %collective-permute-start.10 = (bf16[192,2048]{1,0:T(8,128)(2,1)}, bf16[192,2048]{1,0:T(8,128)(2,1)}, u32[]{:S(2)}, u32[]{:S(2)}) collective-permute-start(bf16[192,2048]{1,0:T(8,128)(2,1)} %collective-permute-done.8), channel_id=1, source_target_pairs={{0,1},{1,0},{2,3},{3,2},{4,5},{5,4},{6,7},{7,6},{8,9},{9,8},{10,11... | collective-permute-start | bytes 2359304 | tf_op jit(solution)/shard_map/ppermute | solution.py:38
  197.7 48.1 %collective-permute-start.2 = (bf16[192,2048]{1,0:T(8,128)(2,1)}, bf16[192,2048]{1,0:T(8,128)(2,1)}, u32[]{:S(2)}, u32[]{:S(2)}) collective-permute-start(bf16[192,2048]{1,0:T(8,128)(2,1)} %collective-permute-done), channel_id=1, source_target_pairs={{0,1},{1,0},{2,3},{3,2},{4,5},{5,4},{6,7},{7,6},{8,9},{9,8},{10,11... | collective-permute-start | bytes 2359304 | tf_op jit(solution)/shard_map/ppermute | solution.py:38
  210.0 26.2 %collective-permute-start.16 = (bf16[192,2048]{1,0:T(8,128)(2,1)}, bf16[192,2048]{1,0:T(8,128)(2,1)S(1)}, u32[]{:S(2)}, u32[]{:S(2)}) collective-permute-start(bf16[192,2048]{1,0:T(8,128)(2,1)} %collective-permute-done.14), channel_id=1, source_target_pairs={{0,1},{1,0},{2,3},{3,2},{4,5},{5,4},{6,7},{7,6},{8,9},{9,8},{10,11... | collective-permute-start | bytes 2359304 | tf_op jit(solution)/shard_map/ppermute | solution.py:38
  210.0 48.5 %collective-permute-start.24 = (bf16[384,2048]{1,0:T(8,128)(2,1)S(1)}, bf16[384,2048]{1,0:T(8,128)(2,1)S(1)}, u32[]{:S(2)}, u32[]{:S(2)}) collective-permute-start(bf16[384,2048]{1,0:T(8,128)(2,1)S(1)} %slice.370), channel_id=1, source_target_pairs={{0,1},{1,0},{2,3},{3,2},{4,5},{5,4},{6,7},{7,6},{8,9},{9,8},{10,11... | collective-permute-start | bytes 4718600 | tf_op jit(solution)/shard_map/ppermute | solution.py:38
  236.2 23.4 %collective-permute-start.11 = (bf16[384,2048]{1,0:T(8,128)(2,1)S(1)}, bf16[384,2048]{1,0:T(8,128)(2,1)}, u32[]{:S(2)}, u32[]{:S(2)}) collective-permute-start(bf16[384,2048]{1,0:T(8,128)(2,1)S(1)} %slice.372), channel_id=1, source_target_pairs={{0,1},{1,0},{2,3},{3,2},{4,5},{5,4},{6,7},{7,6},{8,9},{9,8},{10,11... | collective-permute-start | bytes 4718600 | tf_op jit(solution)/shard_map/ppermute | solution.py:38
  259.1 72.9 %collective-permute-start.25 = (bf16[192,2048]{1,0:T(8,128)(2,1)S(1)}, bf16[192,2048]{1,0:T(8,128)(2,1)S(1)}, u32[]{:S(2)}, u32[]{:S(2)}) collective-permute-start(bf16[192,2048]{1,0:T(8,128)(2,1)S(1)} %slice.374), channel_id=1, source_target_pairs={{0,2},{1,3},{2,0},{3,1},{4,6},{5,7},{6,4},{7,5},{8,10},{9,11},{10,... | collective-permute-start | bytes 2359304 | tf_op jit(solution)/shard_map/ppermute | solution.py:38
  261.6 34.7 %collective-permute-start.12 = (bf16[192,2048]{1,0:T(8,128)(2,1)S(1)}, bf16[192,2048]{1,0:T(8,128)(2,1)S(1)}, u32[]{:S(2)}, u32[]{:S(2)}) collective-permute-start(bf16[192,2048]{1,0:T(8,128)(2,1)S(1)} %slice.376), channel_id=1, source_target_pairs={{0,2},{1,3},{2,0},{3,1},{4,6},{5,7},{6,4},{7,5},{8,10},{9,11},{10,... | collective-permute-start | bytes 2359304 | tf_op jit(solution)/shard_map/ppermute | solution.py:38
  265.3 48.0 %collective-permute-start.19 = (bf16[192,2048]{1,0:T(8,128)(2,1)S(1)}, bf16[192,2048]{1,0:T(8,128)(2,1)S(1)}, u32[]{:S(2)}, u32[]{:S(2)}) collective-permute-start(bf16[192,2048]{1,0:T(8,128)(2,1)S(1)} %slice.375), channel_id=1, source_target_pairs={{0,2},{1,3},{2,0},{3,1},{4,6},{5,7},{6,4},{7,5},{8,10},{9,11},{10,... | collective-permute-start | bytes 2359304 | tf_op jit(solution)/shard_map/ppermute | solution.py:38
  267.8 61.8 %collective-permute-start.5 = (bf16[192,2048]{1,0:T(8,128)(2,1)S(1)}, bf16[192,2048]{1,0:T(8,128)(2,1)S(1)}, u32[]{:S(2)}, u32[]{:S(2)}) collective-permute-start(bf16[192,2048]{1,0:T(8,128)(2,1)S(1)} %slice.377), channel_id=1, source_target_pairs={{0,2},{1,3},{2,0},{3,1},{4,6},{5,7},{6,4},{7,5},{8,10},{9,11},{10,... | collective-permute-start | bytes 2359304 | tf_op jit(solution)/shard_map/ppermute | solution.py:38
  296.6 36.0 %collective-permute-start.13 = (bf16[192,2048]{1,0:T(8,128)(2,1)S(1)}, bf16[192,2048]{1,0:T(8,128)(2,1)S(1)}, u32[]{:S(2)}, u32[]{:S(2)}) collective-permute-start(bf16[192,2048]{1,0:T(8,128)(2,1)S(1)} %fusion.69), channel_id=1, source_target_pairs={{0,4},{1,5},{2,6},{3,7},{4,8},{5,9},{6,10},{7,11},{8,12},{9,13},{1... | collective-permute-start | bytes 2359304 | tf_op jit(solution)/shard_map/ppermute | solution.py:43
  313.5 37.6 %collective-permute-start.20 = (bf16[192,2048]{1,0:T(8,128)(2,1)S(1)}, bf16[192,2048]{1,0:T(8,128)(2,1)S(1)}, u32[]{:S(2)}, u32[]{:S(2)}) collective-permute-start(bf16[192,2048]{1,0:T(8,128)(2,1)S(1)} %fusion.68), channel_id=1, source_target_pairs={{0,8},{1,9},{2,10},{3,11},{4,12},{5,13},{6,14},{7,15},{8,0},{9,1},... | collective-permute-start | bytes 2359304 | tf_op jit(solution)/shard_map/ppermute | solution.py:43
  329.9 36.1 %collective-permute-start.6 = (bf16[192,2048]{1,0:T(8,128)(2,1)S(1)}, bf16[192,2048]{1,0:T(8,128)(2,1)S(1)}, u32[]{:S(2)}, u32[]{:S(2)}) collective-permute-start(bf16[192,2048]{1,0:T(8,128)(2,1)S(1)} %fusion.70), channel_id=1, source_target_pairs={{0,12},{1,13},{2,14},{3,15},{4,0},{5,1},{6,2},{7,3},{8,4},{9,5},{1... | collective-permute-start | bytes 2359304 | tf_op jit(solution)/shard_map/ppermute | solution.py:43
  (68 other events, 932.8 us)
